TPU v7x, 128 devices: a whole 4x4x4 slice. The times are simulated.
128 devices in a mesh: cand: 8 (over y, core), hist: 16 (over z, x).
Axes of the slice: x: 4, y: 4, z: 4, core: 2. Of those that a mesh axis runs over, the one named last changes fastest.
Arguments:
- cand_x: bfloat16 [512, 128, 1024], P(('cand', 'hist')), may hold values from -6 to 6
- w_query: bfloat16 [1024, 1024], replicated, may hold values from -0.1875 to 0.1875
- w_gate: bfloat16 [1024, 1024], replicated, may hold values from -0.1875 to 0.1875
- w_out: bfloat16 [1024, 1024], replicated, may hold values from -0.1875 to 0.1875
- history_kv: bfloat16 [16, 48, 128, 2048], P('cand', 'hist')
- tile_user: int32 [512], P('cand'), may hold values from 0 to 15, as said below
- user_row: int32 [16], replicated, may hold values from 0 to 15, as said below
- hist_len: int32 [16], replicated, may hold values from 1 to 6144, as said below
- pattern: int32 [512, 48], P('cand', 'hist'), may hold values 0 or 1
Outputs:
- mixed: bfloat16 [512, 128, 1024], P(('cand', 'hist'))
Inputs may be any that keep to these rules, and one draw needn't show every extreme that they name: `tile_user`: the tiles of each index of cand (64 consecutive tiles) name, among the 2 cache rows of each index of cand (rows k * 2 to k * 2 + 1 for index k), exactly 1. `user_row`: each cache row is used by exactly one user. `hist_len`: some user has exactly 6144 actions.
All inputs are finite; a program needn't handle non-finite values. No bound on the sum of `pattern` on one device may be relied on, other than what follows from the above.
Results may differ from a plain program's by a relative error of at most 0.013.
Values may be sent and summed in bfloat16 or wider, within the bound.
A program may use at most 192 MiB of HBM per device.

v0:
```python
import functools

import jax
import jax.numpy as jnp
from jax import lax
from jax.experimental import pallas as pl
from jax.experimental.pallas import tpu as pltpu
from jax.sharding import PartitionSpec as P

DH = 128
RING = 4
CORES = 2
QUAD = 4
MESH = pl.DeviceIdType.MESH
DIRECT_QUERIES = ()
DIRECT_SUMS = (7,)

norm_epsilon = 1e-05


STEPS = (
    ("kv_own", "kv_next", "kv_far", "q_own", "q_next", "q_line", "q_line_next")
    + ("compute0", "compute1", "compute2", "rs_one", "rs_two", "rs_three", "rs_four", "rs_five")
    + ("route", "gate_load", "gate")
)
ORDER = (
    24, 25, 0, 26, 27, 32, 33, 1, 28, 29, 34, 40, 41, 8, 36, 30,
    128, 35, 9, 37, 48, 16, 49, 3, 2, 120, 42, 17, 43, 4, 44, 56,
    64, 72, 80, 57, 51, 65, 73, 81, 88, 45, 10, 50, 11, 5, 12, 38,
    89, 31, 52, 18, 6, 7, 136, 19, 96, 58, 66, 74, 82, 97, 59, 67,
    39, 53, 75, 83, 90, 105, 13, 14, 20, 104, 91, 112, 22, 21, 47, 15,
    98, 60, 68, 46, 76, 113, 99, 84, 61, 69, 106, 107, 77, 85, 92, 54,
    23, 93, 114, 115, 55, 100, 62, 70, 78, 86, 101, 63, 71, 79, 87, 94,
    108, 95, 116, 102, 109, 117, 103, 110, 118, 119,
)


def layer_kernel(
    user_row_ref,
    hist_len_ref,
    tile_user_ref,
    pattern_ref,
    cand_ref,
    w_query_ref,
    w_gate_ref,
    w_out_ref,
    history_ref,
    mixed_ref,
    *scratch,
    heads,
    quads,
    tiles_here,
    block_len,
    model_width,
    span,
):
    scratch = list(scratch)

    def take(count):
        taken = scratch[:count]
        del scratch[:count]
        return taken

    kv = take(heads)
    q = take(heads)
    osort = take(2)
    s1, s2p, s2m, r1a, r1b, r2m, r2p, keep = [take(2) for _ in range(8)]
    t1, t2p, t2m = [take(2) for _ in range(3)]
    u1, u2m, u2p = [take(2 + len(DIRECT_SUMS)) for _ in range(3)]
    x_in, weight, gate_act, mixing, squares, open_ref, table, table_smem = take(8)
    local_sem, send_sem, recv_sem = take(3)

    cand = lax.axis_index("cand")
    hist = lax.axis_index("hist")
    y, core = cand // CORES, cand % CORES
    z, x = hist // RING, hist % RING
    xp, xm, xo = (x + 1) % RING, (x + RING - 1) % RING, (x + 2) % RING
    zp, zm, zo = (z + 1) % RING, (z + RING - 1) % RING, (z + 2) % RING
    yp, ym, yo = [((y + d) % RING) * CORES + core for d in (1, RING - 1, 2)]
    dev_yp, dev_ym = (yp, hist), (ym, hist)
    dev_sib = (y * CORES + (CORES - 1 - core), hist)
    dev_xp, dev_xm = (cand, z * RING + xp), (cand, z * RING + xm)
    dev_zp, dev_zm = (cand, zp * RING + x), (cand, zm * RING + x)

    dev_xo, dev_zo = (cand, z * RING + xo), (cand, zo * RING + x)

    barrier = pltpu.get_barrier_semaphore()
    everyone = (dev_yp, dev_ym, dev_sib, dev_xp, dev_xm, dev_xo, dev_zp, dev_zm, dev_zo)
    for device in everyone:
        pl.semaphore_signal(barrier, inc=1, device_id=device, device_id_type=MESH)

    sends = {}
    per_head = 24

    def remote(src, dst, key, device):
        name, h = key
        number = h * per_head + KEYS.index(name)
        return pltpu.make_async_remote_copy(
            src_ref=src,
            dst_ref=dst,
            send_sem=send_sem.at[number],
            recv_sem=recv_sem.at[number],
            device_id=device,
            device_id_type=MESH,
        )

    def send(src, dst, name, h, device):
        copy = remote(src, dst, (name, h), device)
        copy.start()
        sends[(name, h)] = copy

    def arrive(dst, name, h):
        remote(dst, dst, (name, h), dev_sib).wait_recv()

    def sent(name, h):
        copy = sends.pop((name, h), None)
        if copy is not None:
            copy.wait_send()

    def own_copies(h):
        cols = pl.ds(h * DH, DH)
        value_cols = pl.ds((heads + h) * DH, DH)
        rows = 2
        copies = []
        for k, columns in enumerate((cols, value_cols)):
            copies.append(
                pltpu.make_async_copy(
                    history_ref.at[:, :, columns],
                    kv[h].at[pl.ds(cand * rows, rows), k],
                    local_sem.at[h * 2 + k],
                )
            )
        return copies

    def fetch(src, dst, number):
        return pltpu.make_async_copy(src, dst, local_sem.at[2 * heads + number])

    fetched = [
        fetch(cand_ref, x_in, 0),
        fetch(w_query_ref, weight, 1),
        fetch(w_gate_ref, weight, 2),
        fetch(table, table_smem, 3),
        fetch(w_out_ref, weight, 4),
    ]
    fetched[0].start()
    fetched[1].start()
    own = [own_copies(h) for h in range(heads)]
    for h in range(heads):
        for copy in own[h]:
            copy.start()
    fetched[0].wait()
    fetched[1].wait()

    def silu(v):
        return 0.5 * v + 0.5 * v * jnp.tanh(0.5 * v)

    def project(first, width):
        rows = x_in[...].reshape(tiles_here * block_len, model_width)
        product = jnp.dot(
            rows, weight[:, first : first + width], preferred_element_type=jnp.float32
        )
        return silu(product).astype(jnp.bfloat16)

    def project_pair(h):
        both = project(h * DH, 2 * DH)
        for n in range(2):
            mine = both[:, n * DH : (n + 1) * DH].reshape(tiles_here, block_len, DH)
            q[h + n][z, pl.ds(x * tiles_here, tiles_here)] = mine

    project_pair(0)
    pl.semaphore_wait(barrier, len(everyone))

    def gate_load(h):
        fetched[2].start()

    def gate(h):
        fetched[2].wait()
        width = 2 * DH
        for first in range(0, model_width, width):
            gate_act[:, first : first + width] = project(first, width)
        fetched[4].start()

    def route(h):
        tile_count = tile_user_ref.shape[1]
        i32 = jnp.int32
        tile_user = tile_user_ref[...]
        rows = jnp.zeros_like(tile_user)
        lengths = jnp.zeros_like(tile_user)
        for user in range(user_row_ref.shape[0]):
            hit = tile_user == user
            rows = jnp.where(hit, user_row_ref[user], rows)
            lengths = jnp.where(hit, hist_len_ref[user], lengths)
        square = (tile_count, tile_count)
        down, along = lax.broadcasted_iota(i32, square, 0), lax.broadcasted_iota(i32, square, 1)

        def column(v):
            return jnp.sum(
                jnp.where(down == along, jnp.broadcast_to(v, square), 0), axis=1, keepdims=True
            )

        rank = jnp.sum(
            jnp.where((column(rows) == rows) & (down < along), 1, 0), axis=0, keepdims=True
        )
        row_ids = lax.broadcasted_iota(i32, (user_row_ref.shape[0], tile_count), 0)
        count = jnp.sum(jnp.where(row_ids == rows, 1, 0), axis=1, keepdims=True)
        need = lax.shift_right_logical(count + (QUAD - 1), jnp.full_like(count, 2))
        first = jnp.sum(jnp.where(row_ids < rows, need, 0), axis=0, keepdims=True)
        tile_slot = QUAD * first + rank
        wide = (tile_count, table.shape[1])
        slot_tile = jnp.sum(
            jnp.where(
                column(tile_slot) == lax.broadcasted_iota(i32, wide, 1),
                lax.broadcasted_iota(i32, wide, 0),
                0,
            ),
            axis=0,
            keepdims=True,
        )
        table[...] = jnp.zeros_like(table)
        table[0:1, :] = slot_tile
        table[1:2, 0:tile_count] = tile_slot
        table[2:3, 0:tile_count] = rows
        fetched[3].start()
        positions = hist * span + lax.broadcasted_iota(i32, (tile_count, span), 1)
        pattern = pattern_ref[...]
        block_open = jnp.concatenate(
            [
                jnp.broadcast_to(column(pattern[b : b + 1, :]), (tile_count, block_len))
                for b in range(pattern.shape[0])
            ],
            axis=1,
        )
        length = jnp.broadcast_to(column(lengths), (tile_count, span))
        allowed = (positions < length) & (block_open > 0)
        open_ref[...] = jnp.where(allowed, 1.0 / length.astype(jnp.float32), 0.0)
        fetched[3].wait()

    def pair_of(owner):
        return pl.ds(owner * 2, 2)

    other = 1 - 2 * core

    def kv_own(h):
        own[h][0].wait()
        own[h][1].wait()
        mine = kv[h].at[pair_of(cand)]
        send(mine, mine, "kv+", h, dev_yp)
        send(mine, mine, "kv-", h, dev_ym)
        send(mine, mine, "kvs0", h, dev_sib)

    def kv_next(h):
        below, above = kv[h].at[pair_of(ym)], kv[h].at[pair_of(yp)]
        arrive(below, "kv+", h)
        first = kv[h].at[ym * 2]
        send(first, first, "kvf+", h, dev_yp)
        send(below, below, "kvs1", h, dev_sib)
        arrive(above, "kv-", h)
        second = kv[h].at[yp * 2 + 1]
        send(second, second, "kvf-", h, dev_ym)
        send(above, above, "kvs2", h, dev_sib)

    def kv_far(h):
        arrive(kv[h].at[yo * 2], "kvf+", h)
        arrive(kv[h].at[yo * 2 + 1], "kvf-", h)
        far = kv[h].at[pair_of(yo)]
        send(far, far, "kvs3", h, dev_sib)

    def kv_ready(h):
        for number, owner in enumerate((cand, ym, yp, yo)):
            arrive(kv[h].at[pair_of(owner + other)], "kvs%d" % number, h)

    def slot(h, zz, xx, start=0, size=tiles_here):
        return q[h].at[zz, pl.ds(xx * tiles_here + start, size)]

    half = tiles_here // 2

    def q_own(h):
        if h % 2 == 0 and h > 0:
            project_pair(h)
        mine = slot(h, z, x)
        first = h % 2 == 0
        send(mine, mine, "q+", h, dev_xp if first else dev_zp)
        send(mine, mine, "q-", h, dev_xm if first else dev_zm)
        if h in DIRECT_QUERIES:
            send(mine, mine, "qf+", h, dev_xo if first else dev_zo)

    def q_next(h):
        if h % 2 == 0:
            low, high, dp, dm = (z, xm), (z, xp), dev_xp, dev_xm
        else:
            low, high, dp, dm = (zm, x), (zp, x), dev_zp, dev_zm
        arrive(slot(h, *low), "q+", h)
        part = slot(h, *low, 0, half)
        send(part, part, "qf+", h, dp)
        arrive(slot(h, *high), "q-", h)
        part = slot(h, *high, half, half)
        send(part, part, "qf-", h, dm)

    def line(h, at, part=None):
        if h % 2 == 0:
            width = RING * tiles_here
            begin, size = {None: (0, width), 0: (0, width // 2), 1: (width // 2, width // 2)}[part]
            return q[h].at[at, pl.ds(begin, size)]
        begin, size = {None: (0, RING), 0: (0, RING // 2), 1: (RING // 2, RING // 2)}[part]
        return q[h].at[pl.ds(begin, size), pl.ds(at * tiles_here, tiles_here)]

    def q_line(h):
        first = h % 2 == 0
        far = (z, xo) if first else (zo, x)
        if h in DIRECT_QUERIES:
            arrive(slot(h, *((z, xm) if first else (zm, x))), "q+", h)
            arrive(slot(h, *((z, xp) if first else (zp, x))), "q-", h)
            arrive(slot(h, *far), "qf+", h)
        else:
            arrive(slot(h, *far, 0, half), "qf+", h)
            arrive(slot(h, *far, half, half), "qf-", h)
        at, dp, dm = (z, dev_zp, dev_zm) if h % 2 == 0 else (x, dev_xp, dev_xm)
        mine = line(h, at)
        send(mine, mine, "l+", h, dp)
        send(mine, mine, "l-", h, dm)

    def q_line_next(h):
        low, high, dp, dm = (zm, zp, dev_zp, dev_zm) if h % 2 == 0 else (xm, xp, dev_xp, dev_xm)
        arrive(line(h, low), "l+", h)
        part = line(h, low, 0)
        send(part, part, "lf+", h, dp)
        arrive(line(h, high), "l-", h)
        part = line(h, high, 1)
        send(part, part, "lf-", h, dm)

    def q_ready(h):
        far = zo if h % 2 == 0 else xo
        arrive(line(h, far, 0), "lf+", h)
        arrive(line(h, far, 1), "lf-", h)

    half_scale = 0.5 / DH**0.5

    def quad(h, number):
        tiles = [table_smem[0, number * QUAD + a] for a in range(QUAD)]
        row = table_smem[2, tiles[0]]
        group = RING * tiles_here
        block = jnp.concatenate([q[h][t // group, t % group] for t in tiles], axis=0)
        scores = lax.dot_general(
            block, kv[h][row, 0], (((1,), (1,)), ((), ())), preferred_element_type=jnp.float32
        )
        weights = []
        for a in range(QUAD):
            part = (scores[a * DH : (a + 1) * DH] * half_scale).astype(jnp.bfloat16)
            weights.append((part + part * jnp.tanh(part)) * open_ref[pl.ds(tiles[a], 1), :].astype(jnp.bfloat16))
        out = jnp.dot(
            jnp.concatenate(weights, axis=0), kv[h][row, 1], preferred_element_type=jnp.float32
        ).astype(jnp.bfloat16)
        for a in range(QUAD):
            osort[h % 2][number * QUAD + a] = out[a * DH : (a + 1) * DH]

    third = (quads + 2) // 3
    cuts = (0, third, 2 * third, quads)
    unroll = 4

    def compute(part, h):
        if part == 0:
            kv_ready(h)
            q_ready(h)
        first, last = cuts[part], cuts[part + 1]
        whole = (last - first) // unroll

        def body(i, carry):
            for j in range(unroll):
                quad(h, first + i * unroll + j)
            return carry

        lax.fori_loop(0, whole, body, 0)
        for number in range(first + whole * unroll, last):
            quad(h, number)

    def tile_at(h, at, j, i):
        return ((j * RING + at) if h % 2 == 0 else (at * RING + j)) * tiles_here + i

    def partial(h, at, j, i):
        return osort[h % 2][table_smem[1, tile_at(h, at, j, i)]]

    def each_tile(body, first=0, last=RING):
        def step(n, carry):
            for i in range(tiles_here):
                body(n, i)
            return carry

        lax.fori_loop(first, last, step, 0)

    f32 = jnp.float32
    b16 = jnp.bfloat16

    def axis_one(h):
        return (x, xp, xm, xo, dev_xp, dev_xm) if h % 2 == 0 else (z, zp, zm, zo, dev_zp, dev_zm)

    def axis_two(h):
        return axis_one(h + 1)

    def rs_one(h):
        e = h % 2
        at, up, down, far, dp, dm = axis_one(h)
        for name in ("a+", "a-"):
            sent(name, h - 2)

        def body(j, i):
            s1[e][j, i] = partial(h, far, j, i)

        each_tile(body)
        send(s1[e].at[pl.ds(0, 2)], r1a[e], "a+", h, dp)
        send(s1[e].at[pl.ds(2, 2)], r1b[e], "a-", h, dm)

    def rs_two(h):
        e = h % 2
        at, up, down, far, dp, dm = axis_one(h)
        arrive(r1a[e], "a+", h)
        arrive(r1b[e], "a-", h)
        for name in ("b+", "b-"):
            sent(name, h - 2)

        def low(j, i):
            s2p[e][j, i] = (partial(h, up, j, i).astype(f32) + r1a[e][j, i].astype(f32)).astype(b16)
            s2m[e][j, i] = partial(h, down, j, i)

        def high(j, i):
            s2p[e][j, i] = partial(h, up, j, i)
            s2m[e][j, i] = (
                partial(h, down, j, i).astype(f32) + r1b[e][j - 2, i].astype(f32)
            ).astype(b16)

        each_tile(low, 0, 2)
        each_tile(high, 2, 4)
        send(s2p[e], r2m[e], "b+", h, dp)
        send(s2m[e], r2p[e], "b-", h, dm)

    def landing(h):
        return 2 + DIRECT_SUMS.index(h) if h in DIRECT_SUMS else h % 2

    def rs_three(h):
        e = h % 2
        u = landing(h)
        at = axis_one(h)[0]
        _, up, down, far, dp, dm = axis_two(h)
        arrive(r2m[e], "b+", h)
        arrive(r2p[e], "b-", h)
        for name in ("c+", "c-"):
            sent(name, h - 2)

        def body(j, i):
            keep[e][j, i] = (
                partial(h, at, j, i).astype(f32)
                + r2m[e][j, i].astype(f32)
                + r2p[e][j, i].astype(f32)
            ).astype(keep[e].dtype)

        each_tile(body)
        for i in range(tiles_here):
            t1[e][i] = keep[e][far, i].astype(b16)
        if h not in DIRECT_SUMS:
            send(t1[e].at[pl.ds(0, half)], u1[u].at[pl.ds(0, half)], "c+", h, dp)
            send(t1[e].at[pl.ds(half, half)], u1[u].at[pl.ds(half, half)], "c-", h, dm)
            return
        for name in ("d+", "d-"):
            sent(name, h - 2)
        for i in range(tiles_here):
            t2p[e][i] = keep[e][up, i].astype(b16)
            t2m[e][i] = keep[e][down, i].astype(b16)
        send(t2p[e], u2m[u], "d+", h, dp)
        send(t2m[e], u2p[u], "d-", h, dm)
        send(t1[e], u1[u], "c+", h, dev_zo if h % 2 == 0 else dev_xo)

    def rs_four(h):
        e = h % 2
        u = landing(h)
        _, up, down, _, dp, dm = axis_two(h)
        arrive(u1[u].at[pl.ds(0, half)], "c+", h)
        arrive(u1[u].at[pl.ds(half, half)], "c-", h)
        for name in ("d+", "d-"):
            sent(name, h - 2)
        for i in range(tiles_here):
            to_up, to_down = keep[e][up, i].astype(f32), keep[e][down, i].astype(f32)
            if i < half:
                to_up = to_up + u1[u][i].astype(f32)
            else:
                to_down = to_down + u1[u][i].astype(f32)
            t2p[e][i] = to_up.astype(b16)
            t2m[e][i] = to_down.astype(b16)
        send(t2p[e], u2m[u], "d+", h, dp)
        send(t2m[e], u2p[u], "d-", h, dm)

    def rs_five(h):
        e = h % 2
        u = landing(h)
        at = axis_two(h)[0]
        arrive(u2m[u], "d+", h)
        arrive(u2p[u], "d-", h)
        direct = h in DIRECT_SUMS
        if direct:
            arrive(u1[u], "c+", h)
        cols = slice(h * DH, (h + 1) * DH)
        total = keep[e][at].astype(f32) + u2m[u][...].astype(f32) + u2p[u][...].astype(f32)
        if direct:
            total = total + u1[u][...].astype(f32)
        total = total.reshape(tiles_here * block_len, DH)
        hidden = (total * gate_act[:, cols].astype(f32)).astype(b16)
        if not mixed_heads:
            fetched[4].wait()
        for first in range(0, model_width, 2 * DH):
            wide = slice(first, first + 2 * DH)
            product = jnp.dot(hidden, weight[cols, wide], preferred_element_type=f32)
            mixing[:, wide] = mixing[:, wide] + product if mixed_heads else product
        squares[...] = squares[...] + total * total if mixed_heads else total * total
        mixed_heads.append(h)

    mixed_heads = []

    def finish():
        mean_square = jnp.sum(squares[...], axis=1, keepdims=True) * (1.0 / model_width)
        scale = lax.rsqrt(mean_square + norm_epsilon)
        for i in range(tiles_here):
            rows = slice(i * block_len, (i + 1) * block_len)
            mixed_ref[i] = (mixing[rows, :] * scale[rows] + x_in[i].astype(f32)).astype(b16)

    run = {
        "kv_own": kv_own,
        "kv_next": kv_next,
        "kv_far": kv_far,
        "q_own": q_own,
        "q_next": q_next,
        "q_line": q_line,
        "q_line_next": q_line_next,
        "compute0": functools.partial(compute, 0),
        "compute1": functools.partial(compute, 1),
        "compute2": functools.partial(compute, 2),
        "rs_one": rs_one,
        "rs_two": rs_two,
        "rs_three": rs_three,
        "rs_four": rs_four,
        "rs_five": rs_five,
        "route": route,
        "gate_load": gate_load,
        "gate": gate,
    }
    for code in ORDER:
        run[STEPS[code // 8]](code % 8)
    finish()
    for name, h in list(sends):
        sent(name, h)


KEYS = (
    ("kv+", "kv-", "kvf+", "kvf-", "kvs0", "kvs1", "kvs2", "kvs3")
    + ("q+", "q-", "qf+", "qf-", "l+", "l-", "lf+", "lf-")
    + ("a+", "a-", "b+", "b-", "c+", "c-", "d+", "d-")
)


def layer(user_row, hist_len, tile_user, pattern, cand_x, w_query, w_gate, w_out, history):
    tiles_here, block_len, model_width = cand_x.shape
    heads = model_width // DH
    tile_count = tile_user.shape[1]
    cache_rows = CORES * RING * history.shape[0]
    quads = (tile_count + (QUAD - 1) * cache_rows // 2) // QUAD
    span = history.shape[1]
    b16 = jnp.bfloat16
    tile = (block_len, DH)
    lines = pltpu.VMEM((RING, tiles_here) + tile, b16)
    half_lines = pltpu.VMEM((RING // 2, tiles_here) + tile, b16)
    few = pltpu.VMEM((tiles_here,) + tile, b16)
    scratch = (
        [pltpu.VMEM((cache_rows, 2, span, DH), b16)] * heads
        + [pltpu.VMEM((RING, RING * tiles_here) + tile, b16)] * heads
        + [pltpu.VMEM((quads * QUAD,) + tile, b16)] * 2
        + [lines] * 2
        + [lines] * 4
        + [half_lines] * 4
        + [lines] * 4
        + [lines] * 2
        + [few] * 6
        + [few] * (6 + 3 * len(DIRECT_SUMS))
        + [
            pltpu.VMEM(cand_x.shape, b16),
            pltpu.VMEM(w_query.shape, b16),
            pltpu.VMEM((tiles_here * block_len, model_width), b16),
            pltpu.VMEM((tiles_here * block_len, model_width), jnp.float32),
            pltpu.VMEM((tiles_here * block_len, DH), jnp.float32),
            pltpu.VMEM((tile_count, span), jnp.float32),
            pltpu.VMEM((8, DH), jnp.int32),
            pltpu.SMEM((8, DH), jnp.int32),
            pltpu.SemaphoreType.DMA((heads * 2 + 5,)),
            pltpu.SemaphoreType.DMA((heads * 24,)),
            pltpu.SemaphoreType.DMA((heads * 24,)),
        ]
    )
    smem = pl.BlockSpec(memory_space=pltpu.SMEM)
    vmem = pl.BlockSpec(memory_space=pltpu.VMEM)
    return pl.pallas_call(
        functools.partial(
            layer_kernel,
            heads=heads,
            quads=quads,
            tiles_here=tiles_here,
            block_len=block_len,
            model_width=model_width,
            span=span,
        ),
        in_specs=[smem, smem, vmem, vmem] + [pl.BlockSpec(memory_space=pl.ANY)] * 5,
        out_specs=vmem,
        out_shape=jax.ShapeDtypeStruct(cand_x.shape, b16),
        scratch_shapes=scratch,
        cost_estimate=pl.CostEstimate(
            flops=4 * tile_count * block_len * span * model_width,
            bytes_accessed=2 * history.size,
            transcendentals=tile_count * block_len * span * heads,
        ),
        compiler_params=pltpu.CompilerParams(
            collective_id=0, has_side_effects=True, vmem_limit_bytes=63 * 1024 * 1024
        ),
    )(user_row, hist_len, tile_user, pattern, cand_x, w_query, w_gate, w_out, history)


def per_device(cand_x, w_query, w_gate, w_out, history_kv, tile_user, user_row, hist_len, pattern):
    tiles_here, block_len, model_width = cand_x.shape
    own_rows, blocks_here, _, kv_width = history_kv.shape
    span = blocks_here * block_len
    history = history_kv.reshape(own_rows, span, kv_width)

    return layer(
        user_row, hist_len, tile_user[None, :], pattern.T, cand_x, w_query, w_gate, w_out, history
    )


def solution(mesh):
    return jax.shard_map(
        per_device,
        mesh=mesh,
        in_specs=(
            P(("cand", "hist"), None, None),
            P(),
            P(),
            P(),
            P("cand", "hist", None, None),
            P("cand"),
            P(),
            P(),
            P("cand", "hist"),
        ),
        out_specs=P(("cand", "hist"), None, None),
        check_vma=False,
    )
```

profile of v0, /device:TPU:24, one launch (start us, length us, event | category | flops | bytes accessed | tf_op | source)
XLA Modules:
  0.0 197.5 jit_solution(15134874885383510306)
XLA Ops:
  0.0 195.0 %shard_map.91 = bf16[4,128,1024]{2,1,0:T(8,128)(2,1)} custom-call(s32[16]{0:T(128)} %user_row_ref.1, s32[16]{0:T(128)} %hist_len_ref.1, s32[1,64]{1,0:T(1,128)} %bitcast.5, s32[3,64]{1,0:T(4,128)} %bitcast.4, bf16[4,128,1024]{2,1,0:T(8,128)(2,1)} %cand_ref.1, bf16[1024,1024]{1,0:T(8,128)(2,1)} %w_query_ref.1, bf16[1024,1024]{1,0:T(8,128)(2,1)} %w_gate_ref.1, ...), custom_call_target="tpu_custom_call" | custom-call | flops 12884901888 | bytes 3145728 | tf_op jit(solution)/shard_map/pallas_call | solution.py:596
  195.0 2.3 %copy.11 = bf16[4,128,1024]{2,1,0:T(8,128)(2,1)} copy(bf16[4,128,1024]{2,1,0:T(8,128)(2,1)} %shard_map.91) | data formatting | bytes 2097152
where the time goes:
time: 200 us; the launch traced here: 198 us
  Pallas kernels  195 us (98%)
  local copies, waits for them, and re-layouts  2.26 us (1%)
    pallas_call x1, Pallas kernels, layer(): pl.pallas_call(functools.partial(layer_kernel, heads=heads, quads=quads,...  195 us

commit v1 on v0

--- a/solution.py
+++ b/solution.py
@@ -12,6 +12,7 @@
 CORES = 2
 QUAD = 4
 MESH = pl.DeviceIdType.MESH
+OWN_ROWS = 2
 DIRECT_QUERIES = ()
 DIRECT_SUMS = (7,)
 
@@ -24,14 +25,14 @@
     + ("route", "gate_load", "gate")
 )
 ORDER = (
-    24, 25, 0, 26, 27, 32, 33, 1, 28, 29, 34, 40, 41, 8, 36, 30,
-    128, 35, 9, 37, 48, 16, 49, 3, 2, 120, 42, 17, 43, 4, 44, 56,
-    64, 72, 80, 57, 51, 65, 73, 81, 88, 45, 10, 50, 11, 5, 12, 38,
-    89, 31, 52, 18, 6, 7, 136, 19, 96, 58, 66, 74, 82, 97, 59, 67,
-    39, 53, 75, 83, 90, 105, 13, 14, 20, 104, 91, 112, 22, 21, 47, 15,
-    98, 60, 68, 46, 76, 113, 99, 84, 61, 69, 106, 107, 77, 85, 92, 54,
-    23, 93, 114, 115, 55, 100, 62, 70, 78, 86, 101, 63, 71, 79, 87, 94,
-    108, 95, 116, 102, 109, 117, 103, 110, 118, 119,
+    24, 25, 1, 28, 29, 32, 33, 26, 27, 0, 30, 37, 40, 41, 8, 9,
+    128, 38, 31, 36, 34, 120, 35, 136, 48, 3, 16, 2, 49, 42, 43, 44,
+    56, 17, 64, 72, 11, 80, 57, 10, 50, 51, 65, 73, 88, 4, 18, 5,
+    81, 45, 52, 58, 66, 89, 19, 12, 74, 96, 46, 7, 59, 82, 67, 13,
+    53, 20, 75, 97, 6, 83, 90, 60, 15, 68, 76, 39, 105, 21, 104, 14,
+    91, 47, 61, 112, 69, 22, 98, 84, 113, 77, 54, 55, 99, 23, 85, 106,
+    92, 62, 70, 93, 107, 78, 114, 63, 71, 100, 86, 79, 115, 101, 87, 94,
+    109, 108, 95, 116, 102, 117, 103, 110, 118, 119,
 )
 
 
@@ -63,7 +64,7 @@
 
     kv = take(heads)
     q = take(heads)
-    osort = take(2)
+    osort = take(1) + kv[: heads - 1]
     s1, s2p, s2m, r1a, r1b, r2m, r2p, keep = [take(2) for _ in range(8)]
     t1, t2p, t2m = [take(2) for _ in range(3)]
     u1, u2m, u2p = [take(2 + len(DIRECT_SUMS)) for _ in range(3)]
@@ -117,23 +118,26 @@
         if copy is not None:
             copy.wait_send()
 
+    blocks = span // block_len
+    row_size = 2 * blocks
+
     def own_copies(h):
         cols = pl.ds(h * DH, DH)
         value_cols = pl.ds((heads + h) * DH, DH)
-        rows = 2
         copies = []
-        for k, columns in enumerate((cols, value_cols)):
-            copies.append(
-                pltpu.make_async_copy(
-                    history_ref.at[:, :, columns],
-                    kv[h].at[pl.ds(cand * rows, rows), k],
-                    local_sem.at[h * 2 + k],
+        for r in range(OWN_ROWS):
+            for k, columns in enumerate((cols, value_cols)):
+                copies.append(
+                    pltpu.make_async_copy(
+                        history_ref.at[r, :, :, columns],
+                        kv[h].at[pl.ds((cand * OWN_ROWS + r) * row_size + k * blocks, blocks)],
+                        local_sem.at[(h * OWN_ROWS + r) * 2 + k],
+                    )
                 )
-            )
         return copies
 
     def fetch(src, dst, number):
-        return pltpu.make_async_copy(src, dst, local_sem.at[2 * heads + number])
+        return pltpu.make_async_copy(src, dst, local_sem.at[2 * OWN_ROWS * heads + number])
 
     fetched = [
         fetch(cand_ref, x_in, 0),
@@ -236,13 +240,16 @@
         fetched[3].wait()
 
     def pair_of(owner):
-        return pl.ds(owner * 2, 2)
+        return pl.ds(owner * OWN_ROWS * row_size, OWN_ROWS * row_size)
+
+    def one_of(owner, r):
+        return pl.ds((owner * OWN_ROWS + r) * row_size, row_size)
 
     other = 1 - 2 * core
 
     def kv_own(h):
-        own[h][0].wait()
-        own[h][1].wait()
+        for copy in own[h]:
+            copy.wait()
         mine = kv[h].at[pair_of(cand)]
         send(mine, mine, "kv+", h, dev_yp)
         send(mine, mine, "kv-", h, dev_ym)
@@ -251,17 +258,17 @@
     def kv_next(h):
         below, above = kv[h].at[pair_of(ym)], kv[h].at[pair_of(yp)]
         arrive(below, "kv+", h)
-        first = kv[h].at[ym * 2]
+        first = kv[h].at[one_of(ym, 0)]
         send(first, first, "kvf+", h, dev_yp)
         send(below, below, "kvs1", h, dev_sib)
         arrive(above, "kv-", h)
-        second = kv[h].at[yp * 2 + 1]
+        second = kv[h].at[one_of(yp, 1)]
         send(second, second, "kvf-", h, dev_ym)
         send(above, above, "kvs2", h, dev_sib)
 
     def kv_far(h):
-        arrive(kv[h].at[yo * 2], "kvf+", h)
-        arrive(kv[h].at[yo * 2 + 1], "kvf-", h)
+        arrive(kv[h].at[one_of(yo, 0)], "kvf+", h)
+        arrive(kv[h].at[one_of(yo, 1)], "kvf-", h)
         far = kv[h].at[pair_of(yo)]
         send(far, far, "kvs3", h, dev_sib)
 
@@ -341,17 +348,22 @@
         group = RING * tiles_here
         block = jnp.concatenate([q[h][t // group, t % group] for t in tiles], axis=0)
         scores = lax.dot_general(
-            block, kv[h][row, 0], (((1,), (1,)), ((), ())), preferred_element_type=jnp.float32
+            block,
+            kv[h][pl.ds(row * row_size, blocks)].reshape(span, DH),
+            (((1,), (1,)), ((), ())),
+            preferred_element_type=jnp.float32,
         )
         weights = []
         for a in range(QUAD):
             part = (scores[a * DH : (a + 1) * DH] * half_scale).astype(jnp.bfloat16)
             weights.append((part + part * jnp.tanh(part)) * open_ref[pl.ds(tiles[a], 1), :].astype(jnp.bfloat16))
         out = jnp.dot(
-            jnp.concatenate(weights, axis=0), kv[h][row, 1], preferred_element_type=jnp.float32
+            jnp.concatenate(weights, axis=0),
+            kv[h][pl.ds(row * row_size + blocks, blocks)].reshape(span, DH),
+            preferred_element_type=jnp.float32,
         ).astype(jnp.bfloat16)
         for a in range(QUAD):
-            osort[h % 2][number * QUAD + a] = out[a * DH : (a + 1) * DH]
+            osort[h][number * QUAD + a] = out[a * DH : (a + 1) * DH]
 
     third = (quads + 2) // 3
     cuts = (0, third, 2 * third, quads)
@@ -361,6 +373,8 @@
         if part == 0:
             kv_ready(h)
             q_ready(h)
+            for name in KEYS[:8]:
+                sent(name, h - 1)
         first, last = cuts[part], cuts[part + 1]
         whole = (last - first) // unroll
 
@@ -377,7 +391,7 @@
         return ((j * RING + at) if h % 2 == 0 else (at * RING + j)) * tiles_here + i
 
     def partial(h, at, j, i):
-        return osort[h % 2][table_smem[1, tile_at(h, at, j, i)]]
+        return osort[h][table_smem[1, tile_at(h, at, j, i)]]
 
     def each_tile(body, first=0, last=RING):
         def step(n, carry):
@@ -558,18 +572,19 @@
     tiles_here, block_len, model_width = cand_x.shape
     heads = model_width // DH
     tile_count = tile_user.shape[1]
-    cache_rows = CORES * RING * history.shape[0]
+    cache_rows = CORES * RING * OWN_ROWS
     quads = (tile_count + (QUAD - 1) * cache_rows // 2) // QUAD
-    span = history.shape[1]
+    blocks = history.shape[1]
+    span = blocks * block_len
     b16 = jnp.bfloat16
     tile = (block_len, DH)
     lines = pltpu.VMEM((RING, tiles_here) + tile, b16)
     half_lines = pltpu.VMEM((RING // 2, tiles_here) + tile, b16)
     few = pltpu.VMEM((tiles_here,) + tile, b16)
     scratch = (
-        [pltpu.VMEM((cache_rows, 2, span, DH), b16)] * heads
+        [pltpu.VMEM((cache_rows * 2 * blocks,) + tile, b16)] * heads
         + [pltpu.VMEM((RING, RING * tiles_here) + tile, b16)] * heads
-        + [pltpu.VMEM((quads * QUAD,) + tile, b16)] * 2
+        + [pltpu.VMEM((quads * QUAD,) + tile, b16)]
         + [lines] * 2
         + [lines] * 4
         + [half_lines] * 4
@@ -586,7 +601,7 @@
             pltpu.VMEM((tile_count, span), jnp.float32),
             pltpu.VMEM((8, DH), jnp.int32),
             pltpu.SMEM((8, DH), jnp.int32),
-            pltpu.SemaphoreType.DMA((heads * 2 + 5,)),
+            pltpu.SemaphoreType.DMA((heads * OWN_ROWS * 2 + 5,)),
             pltpu.SemaphoreType.DMA((heads * 24,)),
             pltpu.SemaphoreType.DMA((heads * 24,)),
         ]
@@ -619,13 +634,8 @@
 
 
 def per_device(cand_x, w_query, w_gate, w_out, history_kv, tile_user, user_row, hist_len, pattern):
-    tiles_here, block_len, model_width = cand_x.shape
-    own_rows, blocks_here, _, kv_width = history_kv.shape
-    span = blocks_here * block_len
-    history = history_kv.reshape(own_rows, span, kv_width)
-
     return layer(
-        user_row, hist_len, tile_user[None, :], pattern.T, cand_x, w_query, w_gate, w_out, history
+        user_row, hist_len, tile_user[None, :], pattern.T, cand_x, w_query, w_gate, w_out, history_kv
     )
 
 

time: 200 us -> 193 us (0.965)
  Pallas kernels: 195 us -> 188 us
    pallas_call x1, Pallas kernels: 195 us -> 188 us  [layer(): pl.pallas_call(functools.partial(layer_kernel, heads=heads, quads=quads,...]
where the time goes in v1:
time: 193 us; the launch traced here: 190 us
  Pallas kernels  188 us (97%)
  local copies, waits for them, and re-layouts  2.26 us (1%)
    pallas_call x1, Pallas kernels, layer(): pl.pallas_call(functools.partial(layer_kernel, heads=heads, quads=quads,...  188 us

profile of v1, /device:TPU:24, one launch (start us, length us, event | category | flops | bytes accessed | tf_op | source)
XLA Modules:
  0.0 190.1 jit_solution(11628882439282862183)
XLA Ops:
  0.0 187.6 %shard_map.91 = bf16[4,128,1024]{2,1,0:T(8,128)(2,1)} custom-call(s32[16]{0:T(128)} %user_row_ref.1, s32[16]{0:T(128)} %hist_len_ref.1, s32[1,64]{1,0:T(1,128)} %bitcast.3, s32[3,64]{1,0:T(4,128)} %bitcast.2, bf16[4,128,1024]{2,1,0:T(8,128)(2,1)} %cand_ref.1, bf16[1024,1024]{1,0:T(8,128)(2,1)} %w_query_ref.1, bf16[1024,1024]{1,0:T(8,128)(2,1)} %w_gate_ref.1, ...), custom_call_target="tpu_custom_call" | custom-call | flops 12884901888 | bytes 3145728 | tf_op jit(solution)/shard_map/pallas_call | solution.py:611
  187.6 2.3 %copy.11 = bf16[4,128,1024]{2,1,0:T(8,128)(2,1)} copy(bf16[4,128,1024]{2,1,0:T(8,128)(2,1)} %shard_map.91) | data formatting | bytes 2097152

commit v2 on v1

--- a/solution.py
+++ b/solution.py
@@ -25,14 +25,14 @@
     + ("route", "gate_load", "gate")
 )
 ORDER = (
-    24, 25, 1, 28, 29, 32, 33, 26, 27, 0, 30, 37, 40, 41, 8, 9,
-    128, 38, 31, 36, 34, 120, 35, 136, 48, 3, 16, 2, 49, 42, 43, 44,
-    56, 17, 64, 72, 11, 80, 57, 10, 50, 51, 65, 73, 88, 4, 18, 5,
-    81, 45, 52, 58, 66, 89, 19, 12, 74, 96, 46, 7, 59, 82, 67, 13,
-    53, 20, 75, 97, 6, 83, 90, 60, 15, 68, 76, 39, 105, 21, 104, 14,
-    91, 47, 61, 112, 69, 22, 98, 84, 113, 77, 54, 55, 99, 23, 85, 106,
-    92, 62, 70, 93, 107, 78, 114, 63, 71, 100, 86, 79, 115, 101, 87, 94,
-    109, 108, 95, 116, 102, 117, 103, 110, 118, 119,
+    24, 25, 0, 1, 26, 27, 32, 33, 28, 29, 30, 34, 35, 128, 40, 31,
+    8, 41, 2, 9, 136, 36, 37, 43, 120, 48, 16, 42, 49, 10, 44, 3,
+    4, 56, 17, 5, 64, 72, 38, 80, 57, 65, 51, 50, 18, 73, 88, 81,
+    52, 45, 12, 11, 39, 6, 58, 66, 89, 74, 19, 96, 13, 82, 46, 20,
+    59, 7, 67, 53, 75, 14, 97, 90, 83, 60, 21, 104, 68, 105, 47, 15,
+    54, 76, 91, 22, 61, 112, 69, 98, 84, 77, 23, 62, 55, 113, 99, 85,
+    92, 70, 106, 78, 93, 63, 71, 107, 114, 100, 86, 79, 115, 101, 87, 108,
+    94, 109, 95, 116, 102, 117, 103, 110, 118, 119,
 )
 
 
@@ -141,13 +141,19 @@
 
     fetched = [
         fetch(cand_ref, x_in, 0),
-        fetch(w_query_ref, weight, 1),
+        fetch(w_query_ref.at[:, pl.ds(0, 2 * DH)], weight.at[:, pl.ds(0, 2 * DH)], 1),
         fetch(w_gate_ref, weight, 2),
         fetch(table, table_smem, 3),
         fetch(w_out_ref, weight, 4),
+        fetch(
+            w_query_ref.at[:, pl.ds(2 * DH, model_width - 2 * DH)],
+            weight.at[:, pl.ds(2 * DH, model_width - 2 * DH)],
+            5,
+        ),
     ]
     fetched[0].start()
     fetched[1].start()
+    fetched[5].start()
     own = [own_copies(h) for h in range(heads)]
     for h in range(heads):
         for copy in own[h]:
@@ -173,6 +179,7 @@
 
     project_pair(0)
     pl.semaphore_wait(barrier, len(everyone))
+    later_columns = [fetched[5]]
 
     def gate_load(h):
         fetched[2].start()
@@ -283,6 +290,8 @@
 
     def q_own(h):
         if h % 2 == 0 and h > 0:
+            while later_columns:
+                later_columns.pop().wait()
             project_pair(h)
         mine = slot(h, z, x)
         first = h % 2 == 0
@@ -601,7 +610,7 @@
             pltpu.VMEM((tile_count, span), jnp.float32),
             pltpu.VMEM((8, DH), jnp.int32),
             pltpu.SMEM((8, DH), jnp.int32),
-            pltpu.SemaphoreType.DMA((heads * OWN_ROWS * 2 + 5,)),
+            pltpu.SemaphoreType.DMA((heads * OWN_ROWS * 2 + 6,)),
             pltpu.SemaphoreType.DMA((heads * 24,)),
             pltpu.SemaphoreType.DMA((heads * 24,)),
         ]

time: 193 us -> 193 us (level)
  no operation moved by 1% of the time
where the time goes in v2:
time: 193 us; the launch traced here: 189 us
  Pallas kernels  187 us (97%)
  local copies, waits for them, and re-layouts  2.26 us (1%)
    pallas_call x1, Pallas kernels, layer(): pl.pallas_call(functools.partial(layer_kernel, heads=heads, quads=quads,...  187 us

profile of v2, /device:TPU:24, one launch (start us, length us, event | category | flops | bytes accessed | tf_op | source)
XLA Modules:
  0.0 189.3 jit_solution(5649106354260358012)
XLA Ops:
  0.0 186.6 %shard_map.91 = bf16[4,128,1024]{2,1,0:T(8,128)(2,1)} custom-call(s32[16]{0:T(128)} %user_row_ref.1, s32[16]{0:T(128)} %hist_len_ref.1, s32[1,64]{1,0:T(1,128)} %bitcast.3, s32[3,64]{1,0:T(4,128)} %bitcast.2, bf16[4,128,1024]{2,1,0:T(8,128)(2,1)} %cand_ref.1, bf16[1024,1024]{1,0:T(8,128)(2,1)} %w_query_ref.1, bf16[1024,1024]{1,0:T(8,128)(2,1)} %w_gate_ref.1, ...), custom_call_target="tpu_custom_call" | custom-call | flops 12884901888 | bytes 3145728 | tf_op jit(solution)/shard_map/pallas_call | solution.py:620
  186.6 2.3 %copy.11 = bf16[4,128,1024]{2,1,0:T(8,128)(2,1)} copy(bf16[4,128,1024]{2,1,0:T(8,128)(2,1)} %shard_map.91) | data formatting | bytes 2097152
